TPU v7x, 1024 devices: a whole 4x8x16 slice. The times are simulated.
1024 devices in a mesh: scen: 8 (over z_hi, x), shard: 128 (over y, z_lo, core).
Axes of the slice: x: 4, y: 8, z: 16 (z_hi: 2, z_lo: 8; z = z_hi * 8 + z_lo), core: 2. Of those that a mesh axis runs over, the one named last changes fastest.
Arguments:
- layer_input: bfloat16 [262144, 1024], P(('scen', 'shard')), may hold values from -24 to 24
- grad_output: bfloat16 [262144, 1024], P(('scen', 'shard')), may hold values from -6 to 6
- row_counts: int32 [8, 128], P('scen', 'shard'), may hold values from 32 to 256, as said below
- w_shared: bfloat16 [1024, 1024], replicated, may hold values from -0.1875 to 0.1875
- w_scen: bfloat16 [8, 1024, 1024], P('scen'), may hold values from 0.099609375 to 1.8984375
- gain_shared: float32 [1024], replicated, may hold values from 0.25 to 1.75
- gain_scen: float32 [8, 1024], P('scen'), may hold values from 0.25 to 1.75
- saved_mean: float32 [8, 1024], P('scen'), may hold values from -3 to 3
- saved_rstd: float32 [8, 1024], P('scen'), may hold values from 0.5 to 2
- bag_lengths: int32 [1024, 256], P(('scen', 'shard')), may hold values from 1 to 4, 320 in all within a row
- owner_shard: int32 [327680, 1], P(('scen', 'shard')), may hold values from 0 to 127; in each aligned block of 320 rows (0 to 319, 320 to 639, ...) at most 3 rows name the same one
- table_row: int32 [327680], P(('scen', 'shard')), may hold values from 0 to 511
Outputs:
- grad_input: bfloat16 [262144, 1024], P(('scen', 'shard'))
- dw_shared: float32 [1024, 1024], P('shard')
- dw_scen: float32 [8, 1024, 1024], P('scen', 'shard')
- dgain_shared: float32 [1024], replicated
- dgain_scen: float32 [8, 1024], P('scen')
- table_grad: float32 [65536, 128], P('shard')
Inputs may be any that keep to these rules, and one draw needn't show every extreme that they name: `row_counts`: at least 32 live rows on every device; some device holds 256. `bag_lengths`: each of a device's 256 bags holds at least one entry; they sum to 320. `owner_shard`: among the entries of one device no owner appears more than 3 times.
All inputs are finite; a program needn't handle non-finite values.
Results may differ from a plain program's by a relative error of at most 0.015.
Values may be sent and summed in bfloat16 or wider, within the bound.
A program may use at most 64 MiB of HBM per device.

v0:
```python
import jax
import jax.numpy as jnp
from jax import lax
from jax.sharding import PartitionSpec as P

EMB = 128
TROWS_DEV = 512


def route_bags(grad_in, bag_lengths, owner_shard, table_row):
    peer_count = lax.axis_size("shard")
    entries = owner_shard.shape[0]
    slot_cap = max(2, 5 * entries // (4 * peer_count))
    bag_count = grad_in.shape[0]
    pooled = grad_in[:, :EMB]
    bag_ends = jnp.cumsum(bag_lengths[0])
    entry_ids = lax.iota(jnp.int32, entries)
    bag_of = jnp.sum((bag_ends[None, :] <= entry_ids[:, None]).astype(jnp.int32), axis=1)
    picker = (bag_of[:, None] == lax.iota(jnp.int32, bag_count)[None, :]).astype(jnp.bfloat16)
    entry_vals = jnp.dot(picker, pooled, preferred_element_type=jnp.float32).astype(jnp.bfloat16)
    owner_ids = owner_shard[:, 0]
    owner_hot = (owner_ids[:, None] == lax.iota(jnp.int32, peer_count)[None, :]).astype(jnp.int32)
    earlier = jnp.cumsum(owner_hot, axis=0) - owner_hot
    position = jnp.sum(earlier * owner_hot, axis=1)
    slot_ids = owner_ids * slot_cap + position
    placer = slot_ids[:, None] == lax.iota(jnp.int32, peer_count * slot_cap)[None, :]
    send_vals = lax.dot_general(
        placer.astype(jnp.bfloat16),
        entry_vals,
        (((0,), (0,)), ((), ())),
        preferred_element_type=jnp.float32,
    ).astype(jnp.bfloat16)
    send_ids = jnp.sum(jnp.where(placer, table_row[:, None] + 1, 0), axis=0) - 1
    got_vals, got_ids = (
        lax.all_to_all(
            send_vals.reshape(peer_count, slot_cap, EMB),
            "shard",
            split_axis=0,
            concat_axis=0,
            tiled=True,
        ),
        lax.all_to_all(
            send_ids.reshape(peer_count, slot_cap), "shard", split_axis=0, concat_axis=0, tiled=True
        ),
    )
    table_hot = (got_ids.reshape(-1)[:, None] == lax.iota(jnp.int32, TROWS_DEV)[None, :]).astype(
        jnp.bfloat16
    )
    return lax.dot_general(
        table_hot,
        got_vals.reshape(-1, EMB),
        (((0,), (0,)), ((), ())),
        preferred_element_type=jnp.float32,
    )


def reduce_weights(layer_input, grad_pre):
    return lax.psum_scatter(
        lax.dot_general(
            layer_input, grad_pre, (((0,), (0,)), ((), ())), preferred_element_type=jnp.float32
        ),
        "shard",
        scatter_dimension=0,
        tiled=True,
    )


def per_device(
    layer_input,
    grad_output,
    row_counts,
    w_shared,
    w_scen,
    gain_shared,
    gain_scen,
    saved_mean,
    saved_rstd,
    bag_lengths,
    owner_shard,
    table_row,
):
    tok_rows = layer_input.shape[0]
    w_eff = (w_shared.astype(jnp.float32) * w_scen[0].astype(jnp.float32)).astype(jnp.bfloat16)
    pre_norm = jnp.dot(layer_input, w_eff, preferred_element_type=jnp.float32)
    normed = (pre_norm - saved_mean[0]) * saved_rstd[0]
    live_mask = (lax.iota(jnp.int32, tok_rows) < row_counts[0, 0]).astype(jnp.float32)[:, None]
    masked = grad_output.astype(jnp.float32) * live_mask
    total_dy, total_dyx, total_live = lax.psum(
        (
            jnp.sum(masked, axis=0),
            jnp.sum(masked * normed, axis=0),
            row_counts[0, 0].astype(jnp.float32),
        ),
        "shard",
    )
    gain_prod = gain_shared * gain_scen[0]
    grad_pre = (
        live_mask
        * gain_prod
        * saved_rstd[0]
        * (masked - total_dy / total_live - normed * total_dyx / total_live)
    ).astype(jnp.bfloat16)
    grad_in = lax.dot_general(
        grad_pre, w_eff, (((1,), (1,)), ((), ())), preferred_element_type=jnp.float32
    ).astype(jnp.bfloat16)
    weight_rows = reduce_weights(layer_input, grad_pre)
    table_part = route_bags(grad_in, bag_lengths, owner_shard, table_row)
    own_count = weight_rows.shape[0]
    offset = lax.axis_index("shard") * own_count
    shared_block = lax.dynamic_slice_in_dim(w_shared, offset, own_count, 0).astype(jnp.float32)
    scen_block = lax.dynamic_slice_in_dim(w_scen[0], offset, own_count, 0).astype(jnp.float32)
    dw_scen = weight_rows * shared_block
    dw_shared, dgain_shared, table_grad = (
        lax.psum((weight_rows * scen_block).astype(jnp.bfloat16), "scen").astype(jnp.float32),
        lax.psum((gain_scen[0] * total_dyx).astype(jnp.bfloat16), "scen").astype(jnp.float32),
        lax.psum(table_part.astype(jnp.bfloat16), "scen").astype(jnp.float32),
    )
    dgain_scen = gain_shared * total_dyx
    return (grad_in, dw_shared, dw_scen[None], dgain_shared, dgain_scen[None], table_grad)


def solution(mesh):
    placed = (
        P(("scen", "shard"), None),
        P(("scen", "shard"), None),
        P("scen", "shard"),
        P(),
        P("scen", None, None),
        P(),
        P("scen", None),
        P("scen", None),
        P("scen", None),
        P(("scen", "shard"), None),
        P(("scen", "shard"), None),
        P(("scen", "shard")),
    )
    return jax.shard_map(
        per_device,
        mesh=mesh,
        in_specs=placed,
        out_specs=(
            P(("scen", "shard"), None),
            P("shard", None),
            P("scen", "shard", None),
            P(),
            P("scen", None),
            P("shard", None),
        ),
        check_vma=False,
    )
```

profile of v0, /device:TPU:32, one launch (start us, length us, event | category | flops | bytes accessed | tf_op | source)
XLA Modules:
  0.0 1468.0 jit_solution(10977010067324751238)
XLA Ops:
  8.1 0.9 reduce
  9.5 0.7 add_reduce_fusion
  11.1 0.8 sub.39
  11.9 22.7 %all-to-all-start = ((s32[128,1,3]{2,1,0:T(1,128)}), s32[128,1,3]{2,1,0:T(1,128)S(1)}, u32[]{:S(2)}, u32[]{:S(2)}) async-start(s32[128,1,3]{2,1,0:T(1,128)} %bitcast.14), calls=%async_computation | async-start | bytes 131072 | tf_op jit(solution)/shard_map/all_to_all | solution.py:42
  36.2 3.7 fusion.3
  39.9 436.0 %all-reduce.1 = (f32[]{:T(128)}, f32[1024]{0:T(1024)S(1)}, f32[1024]{0:T(1024)S(1)}) all-reduce(f32[]{:T(128)S(6)} %convert_element_type.76, f32[1024]{0:T(1024)S(1)} %get-tuple-element.31, f32[1024]{0:T(1024)S(1)} %get-tuple-element.30), channel_id=1, replica_groups=mesh['scen'=8,'shard'=128] {'shard'}, use_global_device_ids=true, to_apply=%region_2.0 | all-reduce | flops 2049 | bytes 16392 | tf_op jit(solution)/shard_map/psum | solution.py:88
  475.9 1.2 fusion.17
  477.1 4.4 convolution_convert_fusion
  481.6 1.3 convolution_convert_fusion.2
  482.9 0.7 reshape.93
  483.6 8.9 all-to-all-start.1
  493.1 0.8 reduce.8
  494.1 10.3 all-to-all-done.1
  504.5 1.2 convolution_convert_fusion.1
  505.7 4.8 convolution_bitcast_fusion
  510.5 5.3 copy.42
  516.1 0.7 constant_dynamic-slice_fusion.1
  517.0 146.9 %all-reduce.5.cloned.1.call-done = bf16[512,128]{1,0:T(8,128)(2,1)} async-done(((bf16[512,128]{1,0:T(8,128)(2,1)}), bf16[512,128]{1,0:T(8,128)(2,1)}) %all-reduce.5.cloned.1.call-update) | async-done | bytes 131088 | tf_op jit(solution)/shard_map/psum | solution.py:116
  663.9 1.6 convert_element_type.95
  665.5 716.5 %reduce-scatter.4.cloned.1.call-done = f32[8,1024]{1,0:T(8,128)} async-done(((f32[1024,1024]{1,0:T(8,128)}), f32[8,1024]{1,0:T(8,128)}) %reduce-scatter.4.cloned.1.call-update) | async-done | bytes 32784
  1382.0 0.9 copy.43
  1383.1 75.4 %all-reduce.2 = (bf16[8,1024]{0,1:T(8,128)(2,1)S(1)}, bf16[1024]{0:T(1024)(128)(2,1)S(1)}) all-reduce(bf16[8,1024]{0,1:T(8,128)(2,1)S(1)} %get-tuple-element.38, bf16[1024]{0:T(1024)(128)(2,1)S(1)} %get-tuple-element.40), channel_id=1, replica_groups=mesh['scen'=8,'shard'=128] {'scen'}, use_global_device_ids=true, to_apply=%region_6.0 | all-reduce | flops 9216 | bytes 36864 | tf_op jit(solution)/shard_map/psum | solution.py:114
  1458.5 0.7 copy.40
  1459.2 0.8 copy.41
  (47 shorter events, 4.2 us)
Async XLA Ops:
  8.0 28.1 %copy-start = (bf16[256,1024]{1,0:T(8,128)(2,1)S(1)}, bf16[256,1024]{1,0:T(8,128)(2,1)}, u32[]{:S(2)}) copy-start(bf16[256,1024]{1,0:T(8,128)(2,1)} %param.12) | copy-start | bytes 1572868
  8.0 27.3 %copy-start.3 = (s32[1,256]{1,0:T(1,128)S(1)}, s32[1,256]{1,0:T(1,128)}, u32[]{:S(2)}) copy-start(s32[1,256]{1,0:T(1,128)} %param.21) | copy-start | bytes 3076
  8.0 28.1 %copy-start.4 = (bf16[1024,1024]{1,0:T(8,128)(2,1)S(1)}, bf16[1024,1024]{1,0:T(8,128)(2,1)}, u32[]{:S(2)}) copy-start(bf16[1024,1024]{1,0:T(8,128)(2,1)} %param.15) | copy-start | bytes 6291460
  8.0 28.1 %copy-start.7 = (f32[1,1024]{1,0:T(1,128)S(1)}, f32[1,1024]{1,0:T(1,128)}, u32[]{:S(2)}) copy-start(f32[1,1024]{1,0:T(1,128)} %param.20) | copy-start | bytes 12292
  8.0 28.1 %copy-start.6 = (f32[1,1024]{1,0:T(1,128)S(1)}, f32[1,1024]{1,0:T(1,128)}, u32[]{:S(2)}) copy-start(f32[1,1024]{1,0:T(1,128)} %param.19) | copy-start | bytes 12292
  11.9 471.7 %all-to-all-start = ((s32[128,1,3]{2,1,0:T(1,128)}), s32[128,1,3]{2,1,0:T(1,128)S(1)}, u32[]{:S(2)}, u32[]{:S(2)}) async-start(s32[128,1,3]{2,1,0:T(1,128)} %bitcast.14), calls=%async_computation | async-start | bytes 131072 | tf_op jit(solution)/shard_map/all_to_all | solution.py:42
  36.1 439.8 %copy-start.1 = (f32[1024]{0:T(1024)S(1)}, f32[1024]{0:T(1024)}, u32[]{:S(2)}) copy-start(f32[1024]{0:T(1024)} %param.17) | copy-start | bytes 12292
  36.2 439.7 %copy-start.2 = (f32[1,1024]{1,0:T(1,128)S(1)}, f32[1,1024]{1,0:T(1,128)}, u32[]{:S(2)}) copy-start(f32[1,1024]{1,0:T(1,128)} %param.18) | copy-start | bytes 12292
  36.2 441.0 %copy-start.5 = (bf16[256,1024]{1,0:T(8,128)(2,1)S(1)}, bf16[256,1024]{1,0:T(8,128)(2,1)}, u32[]{:S(2)}) copy-start(bf16[256,1024]{1,0:T(8,128)(2,1)} %param.13) | copy-start | bytes 1572868
  483.6 20.8 %all-to-all-start.1 = ((bf16[128,3,128]{2,1,0:T(4,128)(2,1)}), bf16[128,3,128]{2,1,0:T(4,128)(2,1)S(1)}, u32[]{:S(2)}, u32[]{:S(2)}) async-start(bf16[128,3,128]{2,1,0:T(4,128)(2,1)} %reshape.93), calls=%async_computation.1 | async-start | bytes 262144 | tf_op jit(solution)/shard_map/all_to_all | solution.py:35
  492.5 171.4 %all-reduce.5.cloned.1.call-start = ((), (), s32[]{:S(2)}) async-start(), calls=%async_computation.3 | async-start | bytes 262144 | tf_op jit(solution)/shard_map/psum | solution.py:116
  505.7 876.3 %reduce-scatter.4.cloned.1.call-start = ((), (), s32[]{:S(2)}) async-start(), calls=%async_computation.4 | async-start | bytes 4227072
Sparse Core Ops, SparseCore 0:
  505.8 158.0 all-reduce.4
Sparse Core Ops, SparseCore 1:
  516.0 866.0 reduce-scatter.3
where the time goes:
time: 1470 us
  waiting for transfers between devices  874 us (59%)
  blocking collectives  511 us (35%)
  starting transfers between devices  31.7 us (2%)
  between operations  16.4 us (1%)
  matrix products  15.4 us (1%)
    unnamed x3, waiting for transfers between devices  717 us
    psum x1, blocking collectives, per_device(): lax.psum((jnp.sum(masked, axis=0), jnp.sum(masked * normed, axis=0), row_...  436 us
    psum x1, waiting for transfers between devices, per_device(): lax.psum(table_part.astype(jnp.bfloat16), 'scen').astype(jnp.float32)  147 us
    psum x1, blocking collectives, per_device(): lax.psum((weight_rows * scen_block).astype(jnp.bfloat16), 'scen')  75.4 us
  transfers between devices with their start and end apart: 4, of which 3 were waited for; matrix products, arithmetic and copies ran while one was open for 2% of the time, Pallas kernels for 0%

commit v1 on v0

v1 whole, which is shorter than its diff:
```python
import jax
import jax.numpy as jnp
from jax import lax
from jax.experimental import pallas as pl
from jax.experimental.pallas import tpu as pltpu
from jax.sharding import PartitionSpec as P

F32, BF16, I32 = jnp.float32, jnp.bfloat16, jnp.int32
NZH, NX, NY, NZ = 2, 4, 8, 8
ROWS, DIN, DOUT, EMB, TROWS, ENT, CAP = 256, 1024, 1024, 128, 512, 320, 3
HALF = DOUT // 2
LOAD = 256
PART = NZ * CAP
SLOT = 2 * PART
SLOTS = NY * SLOT
TBLK = TROWS // NX
LONG = NY // 2


def remote(src, dst, send, recv, dev):
    return pltpu.make_async_remote_copy(
        src_ref=src,
        dst_ref=dst,
        send_sem=send,
        recv_sem=recv,
        device_id=dev,
        device_id_type=pl.DeviceIdType.MESH,
    )


class Spread:
    def __init__(self, n, me, dev, src_of, buf, sems):
        self.n, self.me, self.dev, self.src_of, self.buf = n, me, dev, src_of, buf
        self.send, self.recv = sems

    def start(self):
        for k in range(1, self.n):
            p = lax.rem(self.me + k, self.n)
            remote(self.src_of(p), self.buf.at[self.me], self.send.at[k], self.recv.at[self.me], self.dev(p)).start()

    def wait(self):
        for k in range(1, self.n):
            q = lax.rem(self.me + k, self.n)
            remote(self.buf.at[q], self.buf.at[q], self.send.at[k], self.recv.at[q], self.dev(q)).wait_recv()

    def finish(self):
        for k in range(1, self.n):
            p = lax.rem(self.me + k, self.n)
            remote(self.src_of(p), self.buf.at[self.me], self.send.at[k], self.recv.at[self.me], self.dev(p)).wait_send()


def nt(a, b):
    return lax.dot_general(a, b, (((1,), (1,)), ((), ())), preferred_element_type=F32)


def nn(a, b):
    return jnp.dot(a, b, preferred_element_type=F32)


def iota(shape, dim):
    return lax.broadcasted_iota(I32, shape, dim)


def hot(cond):
    return jnp.where(cond, 1.0, 0.0).astype(BF16)


def total(buf, n):
    acc = buf[0].astype(F32)
    for i in range(1, n):
        acc = acc + buf[i].astype(F32)
    return acc


def kernel(
    x_hbm, g_hbm, cnt_ref, ws_hbm, wc_hbm, gs_ref, gc_ref, mean_ref, rstd_ref, len_ref, own_ref, row_ref,
    gi_hbm, dws_ref, dwc_ref, dgs_ref, dgc_ref, tab_ref,
    xb, gb, ws, wc, we, nb, gp, xt, gi,
    stat, stat_c, stat_y, stat_z, fin,
    dw, ring, blk, dz, shx, shz,
    meta, meta_p, pick, ids_s, ids_y, ids_t, ids_z, rows_hot, perm,
    val_s, val_y, val_t, val_z, tab_s, tab_x, tab_h, tab_g, dgx, dgh,
    s_load, s_out, s_core, r_core, s_ring, r_ring,
    *spread_sems,
):
    scen, shard = lax.axis_index("scen"), lax.axis_index("shard")
    zh, x = scen // NX, lax.rem(scen, NX)
    y, z, c = shard // (NZ * 2), lax.rem(shard // 2, NZ), lax.rem(shard, 2)

    def dev_y(p):
        return (scen, (p * NZ + z) * 2 + c)

    def dev_z(p):
        return (scen, (y * NZ + p) * 2 + c)

    def dev_x(p):
        return (zh * NX + p, shard)

    def dev_h(p):
        return (p * NX + x, shard)

    other = 1 - c
    partner = (scen, (y * NZ + z) * 2 + other)

    in_x = pltpu.make_async_copy(x_hbm, xb.at[pl.ds(0, ROWS)], s_load.at[0])
    in_g = pltpu.make_async_copy(g_hbm, gb.at[pl.ds(0, ROWS)], s_load.at[1])
    loads = DOUT // LOAD
    in_w = []
    for j in range(loads):
        cols = pl.ds(j * LOAD, LOAD)
        in_w.append((
            pltpu.make_async_copy(ws_hbm.at[:, cols], ws.at[:, cols], s_load.at[2 + 2 * j]),
            pltpu.make_async_copy(wc_hbm.at[:, cols], wc.at[:, cols], s_load.at[3 + 2 * j]),
        ))
    in_x.start()
    for a, b in in_w[:1]:
        a.start()
        b.start()
    in_g.start()
    for a, b in in_w[1:]:
        a.start()
        b.start()

    barrier = pltpu.get_barrier_semaphore()
    peers = [dev_h(1 - zh)]
    peers += [dev_z(lax.rem(z + k, NZ)) for k in range(1, NZ)]
    peers += [dev_y(lax.rem(y + k, NY)) for k in range(1, NY)]
    peers += [dev_x(lax.rem(x + k, NX)) for k in range(1, NX)]
    peers += [partner]
    for p in peers:
        pl.semaphore_signal(barrier, 1, device_id=p, device_id_type=pl.DeviceIdType.MESH)

    sems = [(spread_sems[2 * i], spread_sems[2 * i + 1]) for i in range(len(spread_sems) // 2)]
    go_stat_y = Spread(NY, y, dev_y, lambda p: stat_y.at[y], stat_y, sems[0])
    go_stat_z = Spread(NZ, z, dev_z, lambda p: stat_z.at[z], stat_z, sems[1])
    go_ids_y = Spread(NY, y, dev_y, lambda p: ids_s.at[p], ids_y, sems[2])
    go_ids_z = Spread(NZ, z, dev_z, lambda p: ids_t.at[p], ids_z, sems[3])
    go_val_y = Spread(NY, y, dev_y, lambda p: val_s.at[p], val_y, sems[4])
    go_val_z = Spread(NZ, z, dev_z, lambda p: val_t.at[p], val_z, sems[5])
    go_dw_z = Spread(NZ, z, dev_z, lambda p: blk.at[p], dz, sems[6])
    go_sh_x = Spread(NX, x, dev_x, lambda p: shx.at[x], shx, sems[7])
    go_sh_h = Spread(NZH, zh, dev_h, lambda p: shz.at[zh], shz, sems[8])
    go_tab_x = Spread(NX, x, dev_x, lambda p: tab_s.at[p], tab_x, sems[9])
    go_tab_h = Spread(NZH, zh, dev_h, lambda p: tab_h.at[zh], tab_h, sems[10])
    go_tab_g = Spread(NX, x, dev_x, lambda p: tab_g.at[x], tab_g, sems[11])
    go_dg_x = Spread(NX, x, dev_x, lambda p: dgx.at[x], dgx, sems[12])
    go_dg_h = Spread(NZH, zh, dev_h, lambda p: dgh.at[zh], dgh, sems[13])
    spreads = [go_stat_y, go_stat_z, go_ids_y, go_ids_z, go_val_y, go_val_z, go_dw_z, go_sh_x, go_sh_h,
               go_tab_x, go_tab_h, go_tab_g, go_dg_x, go_dg_h]
    core_stat = remote(stat.at[other], stat_c, s_core.at[0], r_core.at[0], partner)
    core_fin = remote(fin.at[c], fin.at[c], s_core.at[1], r_core.at[1], partner)
    core_fin_in = remote(fin.at[other], fin.at[other], s_core.at[1], r_core.at[1], partner)
    core_meta = remote(meta, meta_p, s_core.at[2], r_core.at[2], partner)
    core_x = remote(x_hbm, xb.at[pl.ds(ROWS, ROWS)], s_core.at[3], r_core.at[3], partner)
    core_g = remote(g_hbm, gb.at[pl.ds(ROWS, ROWS)], s_core.at[4], r_core.at[4], partner)

    own_hot = hot(own_ref[...] == iota((ENT, 128), 1))
    earlier = nn(hot(iota((ENT, ENT), 1) < iota((ENT, ENT), 0)), own_hot) * own_hot.astype(F32)
    place_row = nt(jnp.ones((8, 128), BF16), earlier.astype(BF16))
    owner_row = nt(iota((8, 128), 1).astype(F32).astype(BF16), own_hot)
    meta[...] = jnp.zeros_like(meta)
    meta[0:1, 0:ROWS] = len_ref[...].astype(F32)
    meta[1:2, 0:ENT] = owner_row[0:1] * 4.0 + place_row[0:1]
    meta[2:3, 0:ENT] = row_ref[...].astype(F32)

    count = cnt_ref[0, 0]
    stat[...] = jnp.zeros_like(stat)
    live = iota((ROWS, LOAD), 0) < count
    in_x.wait()
    for j in range(loads):
        cols = pl.ds(j * LOAD, LOAD)
        in_w[j][0].wait()
        in_w[j][1].wait()
        w_j = (ws[:, cols].astype(F32) * wc[:, cols].astype(F32)).astype(BF16)
        we[:, cols] = w_j
        normed = (nn(xb[0:ROWS, :], w_j) - mean_ref[:, cols]) * rstd_ref[:, cols]
        nb[0:ROWS, cols] = normed
        if j == 0:
            in_g.wait()
        masked = jnp.where(live, gb[0:ROWS, cols].astype(F32), 0.0)
        h, at = (j * LOAD) // HALF, (j * LOAD) % HALF
        stat[h, 0:1, at : at + LOAD] = jnp.sum(masked, axis=0, keepdims=True)
        stat[h, 1:2, at : at + LOAD] = jnp.sum(masked * normed, axis=0, keepdims=True)
    cnt_row = jnp.full((1, HALF), count, I32).astype(F32)
    stat[0, 2:3, :] = cnt_row
    stat[1, 2:3, :] = cnt_row

    pl.semaphore_wait(barrier, len(peers))
    core_stat.start()
    core_meta.start()
    core_x.start()
    core_g.start()

    xt_rows = DIN // 2
    choose_i, choose_k = iota((xt_rows, DIN), 0), iota((xt_rows, DIN), 1)
    choose = hot(choose_k == (choose_i >> 3) * 16 + c * 8 + (choose_i & 7))

    core_stat.wait_recv()
    stat_y[y] = stat[c] + stat_c[...]
    go_stat_y.start()

    xt[:, 0:ROWS] = nt(choose, xb[0:ROWS, :]).astype(BF16)

    def slots_of(m, src):
        lens = m[0:1, 0:ROWS]
        upto = hot(iota((ROWS, ROWS), 0) <= iota((ROWS, ROWS), 1))
        ends = nn(jnp.broadcast_to(lens, (8, ROWS)).astype(BF16), upto)[0:1]
        entry = iota((ENT, ROWS), 0).astype(F32)
        picker = hot((ends > entry) & (ends - lens <= entry))
        code = m[1:2, 0:ENT].astype(I32)
        owner, place = code >> 2, code & 3
        inside = src * PART + ((owner >> 1) & 7) * CAP + place
        mine = (owner & 1) == c
        slot = jnp.where(mine, (owner >> 4) * SLOT + inside, -1)
        wide = jnp.where(mine, (owner >> 4) * 128 + inside, -1)
        chosen = nn(hot(iota((SLOTS, ENT), 0) == slot), picker).astype(BF16)
        name = m[2:3, 0:ENT].astype(I32) + 1
        part = jnp.where(iota((8, ENT), 0) == 0, name >> 4, name & 15)
        names = nt(part.astype(F32).astype(BF16), hot(iota((NY * 128, ENT), 0) == wide))
        return chosen, names

    core_meta.wait_recv()
    chosen, names = slots_of(meta, c)
    pick[:, 0:ROWS] = chosen
    chosen, names_p = slots_of(meta_p, other)
    pick[:, ROWS : 2 * ROWS] = chosen
    names = names + names_p
    for i in range(NY):
        ids_s[i] = names[:, i * 128 : (i + 1) * 128]

    go_stat_y.wait()
    stat_z[z] = total(stat_y, NY)
    go_stat_z.start()
    ids_y[y] = ids_s[y]
    go_ids_y.start()

    core_x.wait_recv()
    xt[:, ROWS : 2 * ROWS] = nt(choose, xb[ROWS : 2 * ROWS, :]).astype(BF16)
    for j in range(loads):
        cols = pl.ds(j * LOAD, LOAD)
        nb[ROWS : 2 * ROWS, cols] = (nn(xb[ROWS : 2 * ROWS, :], we[:, cols]) - mean_ref[:, cols]) * rstd_ref[:, cols]
    out_i, in_i = iota((SLOTS, SLOTS), 0), iota((SLOTS, SLOTS), 1)
    to_z = (out_i * 1366) >> 16
    in_z = out_i - to_z * SLOT
    six, from_y = in_z >> 3, in_z & 7
    src_c = jnp.where(six >= CAP, 1, 0)
    perm[...] = hot(in_i == from_y * SLOT + src_c * PART + to_z * CAP + six - CAP * src_c)
    core_g.wait_recv()

    go_stat_z.wait()
    fin[c] = total(stat_z, NZ)
    core_fin.start()
    scale = gs_ref[...] * gc_ref[...] * rstd_ref[...]
    core_fin_in.wait_recv()

    sums = [jnp.concatenate([fin[0, i : i + 1, :], fin[1, i : i + 1, :]], axis=1) for i in range(3)]
    sum_dyx = sums[1]
    mean_dy, mean_dyx = sums[0] / sums[2], sums[1] / sums[2]
    count_p = stat_c[2:3, 0:1]

    step = 64
    for i in range(2 * ROWS // step):
        rows = slice(i * step, (i + 1) * step)
        at = iota((step, 1), 0).astype(F32) + float((i * step) % ROWS)
        if i * step < ROWS:
            alive = at < count.astype(F32)
        else:
            alive = at < count_p
        g = gb[rows, :].astype(F32)
        gp[rows, :] = jnp.where(alive, scale * (g - mean_dy - nb[rows, :] * mean_dyx), 0.0).astype(BF16)

    for j in range(DOUT // LOAD):
        cols = slice(j * LOAD, (j + 1) * LOAD)
        dw[:, :, :, cols] = nn(xt[...], gp[:, cols]).astype(BF16).reshape(NY, 2, 32, LOAD)

    streams = []
    for h in range(2):
        for d in (1, -1):
            streams.append((len(streams), h, d, LONG if (h == 0) == (d == 1) else LONG - 1))

    def hop(s, h, d, n, k):
        src = dw.at[lax.rem(y + d * (n - k) + NY, NY), h] if k == 0 else ring.at[s, k - 1]
        return remote(src, ring.at[s, k], s_ring.at[s, k], r_ring.at[s, k], dev_y(lax.rem(y + d + NY, NY)))

    for s, h, d, n in streams:
        hop(s, h, d, n, 0).start()

    def ring_step(k):
        for s, h, d, n in streams:
            if k < n - 1:
                hop(s, h, d, n, k).wait_recv()
                own = dw[lax.rem(y + d * (n - k - 1) + NY, NY), h]
                ring[s, k] = (ring[s, k].astype(F32) + own.astype(F32)).astype(BF16)
                hop(s, h, d, n, k + 1).start()

    pooled = nt(gp[...], we[0:EMB, :]).astype(BF16)
    val_s[...] = nn(pick[...], pooled).astype(BF16).reshape(NY, SLOT, EMB)
    val_y[y] = val_s[y]
    go_val_y.start()

    dgc_ref[...] = gs_ref[...] * sum_dyx
    gain_term = gc_ref[...] * sum_dyx
    for i in range(8):
        dgx[x, i : i + 1, :] = gain_term[:, i * 128 : (i + 1) * 128]
    go_dg_x.start()

    for j in range(2):
        cols = slice(j * LOAD, (j + 1) * LOAD)
        gi[:, cols] = nt(gp[0:ROWS, :], we[cols, :]).astype(BF16)

    ring_step(0)

    for j in range(2, DIN // LOAD):
        cols = slice(j * LOAD, (j + 1) * LOAD)
        gi[:, cols] = nt(gp[0:ROWS, :], we[cols, :]).astype(BF16)
    out_gi = pltpu.make_async_copy(gi, gi_hbm, s_out.at[0])
    out_gi.start()

    go_ids_y.wait()
    halves = [jnp.concatenate([ids_y[i, r : r + 1, :] for i in range(NY)], axis=0) for r in range(2)]
    q_in, q_out = iota((128, NZ * 128), 0), iota((128, NZ * 128), 1)
    q_z, q_six = q_out >> 7, q_out & 127
    q_src = jnp.where(q_six >= CAP, 1, 0)
    spreader = hot((q_six < 2 * CAP) & (q_in == q_src * PART + q_z * CAP + q_six - CAP * q_src))
    named = nn(jnp.concatenate(halves, axis=0).astype(BF16), spreader)
    named = named[0:8] * 16.0 + named[8:16]
    for i in range(NZ):
        ids_t[i] = named[:, i * 128 : (i + 1) * 128]
    ids_z[z] = ids_t[z]
    go_ids_z.start()

    ring_step(1)

    go_val_y.wait()
    val_t[...] = nn(perm[...], val_y[...].reshape(SLOTS, EMB)).astype(BF16).reshape(NZ, SLOT, EMB)
    val_z[z] = val_t[z]
    go_val_z.start()
    go_dg_x.wait()
    dgh[zh] = total(dgx, NX)
    go_dg_h.start()

    ring_step(2)

    go_ids_z.wait()
    for i in range(NZ):
        for k in range(0, 2 * CAP, 2):
            pair = [ids_z[i][:, t : t + 1] - 1.0 for t in (k, k + 1)]
            at = jnp.concatenate([jnp.broadcast_to(t, (8, TROWS)) for t in pair], axis=0)
            at_row = i * SLOT + k * 8
            rows_hot[at_row : at_row + 16, :] = hot(at == iota((16, TROWS), 1).astype(F32))

    for s, h, d, n in streams:
        hop(s, h, d, n, n - 1).wait_recv()
    for h in range(2):
        long_s, short_s = (0, 1) if h == 0 else (3, 2)
        summed = ring[long_s, LONG - 1].astype(F32) + dw[y, h].astype(F32) + ring[short_s, LONG - 2].astype(F32)
        for i in range(4):
            b = summed[8 * i : 8 * (i + 1)]
            blk[4 * h + i] = jnp.concatenate([b[:, 0:HALF], b[:, HALF:DOUT]], axis=0).astype(BF16)
    dz[z] = blk[z]
    go_dw_z.start()

    go_val_z.wait()
    table = lax.dot_general(
        rows_hot[...], val_z[...].reshape(SLOTS, EMB), (((0,), (0,)), ((), ())), preferred_element_type=F32
    )
    tab_s[...] = table.astype(BF16).reshape(NX, TBLK, EMB)
    tab_x[x] = tab_s[x]
    go_tab_x.start()

    base = pl.multiple_of((y * NZ + z) * 16, 16)

    def block_of(w):
        pair = w[pl.ds(base, 16), :].astype(F32)
        return jnp.where(c == 0, pair[0:8], pair[8:16])

    w_s, w_c = block_of(ws), block_of(wc)

    go_dw_z.wait()
    summed = total(dz, NZ)
    dw_rows = jnp.concatenate([summed[0:8], summed[8:16]], axis=1)
    shared = dw_rows * w_c
    shx[x] = jnp.concatenate([shared[:, 0:HALF], shared[:, HALF:DOUT]], axis=0).astype(BF16)
    go_sh_x.start()
    dwc_ref[...] = dw_rows * w_s

    go_tab_x.wait()
    tab_h[zh] = total(tab_x, NX).astype(BF16)
    go_tab_h.start()

    go_sh_x.wait()
    shz[zh] = total(shx, NX).astype(BF16)
    go_sh_h.start()

    go_dg_h.wait()
    dgs_ref[...] = total(dgh, NZH)

    go_tab_h.wait()
    tab_g[x] = total(tab_h, NZH).astype(BF16)
    go_tab_g.start()

    go_sh_h.wait()
    summed = total(shz, NZH)
    dws_ref[...] = jnp.concatenate([summed[0:8], summed[8:16]], axis=1)

    go_tab_g.wait()
    tab_ref[...] = tab_g[...].astype(F32).reshape(TROWS, EMB)

    for sp in spreads:
        sp.finish()
    for cp in (core_stat, core_fin, core_meta, core_x, core_g):
        cp.wait_send()
    for s, h, d, n in streams:
        for k in range(n):
            hop(s, h, d, n, k).wait_send()
    out_gi.wait()


def per_device(*args):
    (layer_input, grad_output, row_counts, w_shared, w_scen, gain_shared, gain_scen,
     saved_mean, saved_rstd, bag_lengths, owner_shard, table_row) = args
    vm, sm, anywhere = (pl.BlockSpec(memory_space=m) for m in (pltpu.VMEM, pltpu.SMEM, pl.ANY))
    dma = pltpu.SemaphoreType.DMA
    V = pltpu.VMEM
    sizes = [NY, NZ, NY, NZ, NY, NZ, NZ, NX, NZH, NX, NZH, NX, NX, NZH]
    scratch = [
        V((2 * ROWS, DIN), BF16), V((2 * ROWS, DOUT), BF16), V((DIN, DOUT), BF16), V((DIN, DOUT), BF16),
        V((DIN, DOUT), BF16), V((2 * ROWS, DOUT), F32), V((2 * ROWS, DOUT), BF16), V((DIN // 2, 2 * ROWS), BF16),
        V((ROWS, DIN), BF16),
        V((2, 8, HALF), F32), V((8, HALF), F32), V((NY, 8, HALF), F32), V((NZ, 8, HALF), F32), V((2, 8, HALF), F32),
        V((NY, 2, 32, DOUT), BF16), V((4, LONG, 32, DOUT), BF16), V((NZ, 16, HALF), BF16),
        V((NZ, 16, HALF), BF16), V((NX, 16, HALF), BF16), V((NZH, 16, HALF), BF16),
        V((8, 512), F32), V((8, 512), F32), V((SLOTS, 2 * ROWS), BF16), V((NY, 8, 128), F32), V((NY, 8, 128), F32),
        V((NZ, 8, 128), F32), V((NZ, 8, 128), F32), V((SLOTS, TROWS), BF16), V((SLOTS, SLOTS), BF16),
        V((NY, SLOT, EMB), BF16), V((NY, SLOT, EMB), BF16), V((NZ, SLOT, EMB), BF16), V((NZ, SLOT, EMB), BF16),
        V((NX, TBLK, EMB), BF16), V((NX, TBLK, EMB), BF16), V((NZH, TBLK, EMB), BF16), V((NX, TBLK, EMB), BF16),
        V((NX, 8, 128), F32), V((NZH, 8, 128), F32),
        dma((2 + 2 * (DOUT // LOAD),)), dma((1,)), dma((5,)), dma((5,)), dma((4, LONG)), dma((4, LONG)),
    ]
    for n in sizes:
        scratch += [dma((n,)), dma((n,))]
    shape = jax.ShapeDtypeStruct
    grad_in, dw_shared, dw_scen, dgain_shared, dgain_scen, table = pl.pallas_call(
        kernel,
        out_shape=(
            shape((ROWS, DIN), BF16), shape((8, DOUT), F32), shape((8, DOUT), F32),
            shape((8, 128), F32), shape((1, DOUT), F32), shape((TROWS, EMB), F32),
        ),
        in_specs=[anywhere, anywhere, sm, anywhere, anywhere] + [vm] * 7,
        out_specs=(anywhere, vm, vm, vm, vm, vm),
        scratch_shapes=scratch,
        compiler_params=pltpu.CompilerParams(collective_id=0, has_side_effects=True, vmem_limit_bytes=56 << 20),
        name="layer_backward",
    )(
        layer_input, grad_output, row_counts, w_shared, w_scen[0], gain_shared.reshape(1, DOUT), gain_scen,
        saved_mean, saved_rstd, bag_lengths, owner_shard, table_row.reshape(1, ENT),
    )
    return grad_in, dw_shared, dw_scen[None], dgain_shared.reshape(DOUT), dgain_scen, table


def solution(mesh):
    placed = (
        P(("scen", "shard"), None),
        P(("scen", "shard"), None),
        P("scen", "shard"),
        P(),
        P("scen", None, None),
        P(),
        P("scen", None),
        P("scen", None),
        P("scen", None),
        P(("scen", "shard"), None),
        P(("scen", "shard"), None),
        P(("scen", "shard")),
    )
    return jax.shard_map(
        per_device,
        mesh=mesh,
        in_specs=placed,
        out_specs=(
            P(("scen", "shard"), None),
            P("shard", None),
            P("scen", "shard", None),
            P(),
            P("scen", None),
            P("shard", None),
        ),
        check_vma=False,
    )
```

time: 1470 us -> 92.9 us (0.06)
  the two profiles are of different devices: /device:TPU:32 before, /device:TPU:48 now
where the time goes in v1:
time: 92.9 us; the launch traced here: 92.4 us
  Pallas kernels  79.5 us (86%)
  local copies, waits for them, and re-layouts  11.6 us (12%)
  between operations  1.29 us (1%)
    pallas_call x1, Pallas kernels, per_device(): pl.pallas_call(kernel, out_shape=(shape((ROWS, DIN), BF16), shape((8, DOU...  79.5 us
    unnamed x7, local copies, waits for them, and re-layouts  10.3 us

profile of v1, /device:TPU:48, one launch (start us, length us, event | category | flops | bytes accessed | tf_op | source)
XLA Modules:
  0.0 92.4 jit_solution(17648946395688926277)
XLA Ops:
  1.3 1.2 %reshape.22.row_ref = s32[1,320]{1,0:T(1,128)} reshape(s32[320]{0:T(512)} %param.23) | data formatting | bytes 2560 | tf_op jit(solution)/shard_map/reshape | solution.py:456
  2.5 1.5 %copy.18.own_ref = s32[320,1]{1,0:T(8,128)} copy(s32[320,1]{0,1:T(1,128)} %param.22) | data formatting | bytes 2560 | tf_op args[10]
  4.0 79.5 %layer_backward.1 = (bf16[256,1024]{1,0:T(8,128)(2,1)}, f32[8,1024]{1,0:T(8,128)}, f32[8,1024]{1,0:T(8,128)}, f32[8,128]{1,0:T(8,128)}, f32[1,1024]{1,0:T(1,128)}, /*index=5*/f32[512,128]{1,0:T(8,128)}) custom-call(bf16[256,1024]{1,0:T(8,128)(2,1)} %x_hbm.1, bf16[256,1024]{1,0:T(8,128)(2,1)} %g_hbm.1, s32[1,1]{1,0:T(1,128)S(6)} %copy.25.cnt_ref, ...), custom_call_target="tpu_custom_call" | custom-call | tf_op jit(solution)/shard_map/layer_backward/pallas_call | solution.py:443
  83.5 1.9 %copy.26 = bf16[256,1024]{1,0:T(8,128)(2,1)} copy(bf16[256,1024]{1,0:T(8,128)(2,1)} %get-tuple-element.24) | data formatting | bytes 1048576
  85.4 1.4 %copy.27 = f32[8,1024]{1,0:T(8,128)} copy(f32[8,1024]{1,0:T(8,128)} %get-tuple-element.25) | data formatting | bytes 65536
  86.8 1.4 %copy.28 = f32[1,8,1024]{2,1,0:T(8,128)} copy(f32[1,8,1024]{2,1,0:T(8,128)} %bitcast.5) | data formatting | bytes 65536
  88.1 1.3 %copy.29 = f32[1024]{0:T(1024)} copy(f32[1024]{0:T(1024)} %bitcast.6) | data formatting | bytes 8192
  89.4 1.3 %copy.30 = f32[1,1024]{1,0:T(1,128)} copy(f32[1,1024]{1,0:T(1,128)} %get-tuple-element.28) | data formatting | bytes 8192
  90.7 1.7 %copy.31 = f32[512,128]{1,0:T(8,128)} copy(f32[512,128]{1,0:T(8,128)} %get-tuple-element.29) | data formatting | bytes 524288

commit v2 on v1

--- a/solution.py
+++ b/solution.py
@@ -29,9 +29,10 @@
 
 
 class Spread:
-    def __init__(self, n, me, dev, src_of, buf, sems):
+    def __init__(self, n, me, dev, src_of, buf, sems, by_place=False):
         self.n, self.me, self.dev, self.src_of, self.buf = n, me, dev, src_of, buf
         self.send, self.recv = sems
+        self.by_place = by_place
 
     def start(self):
         for k in range(1, self.n):
@@ -46,7 +47,8 @@
     def finish(self):
         for k in range(1, self.n):
             p = lax.rem(self.me + k, self.n)
-            remote(self.src_of(p), self.buf.at[self.me], self.send.at[k], self.recv.at[self.me], self.dev(p)).wait_send()
+            sem = self.send.at[p if self.by_place else k]
+            remote(self.src_of(p), self.buf.at[self.me], sem, self.recv.at[self.me], self.dev(p)).wait_send()
 
 
 def nt(a, b):
@@ -137,7 +139,7 @@
     go_ids_z = Spread(NZ, z, dev_z, lambda p: ids_t.at[p], ids_z, sems[3])
     go_val_y = Spread(NY, y, dev_y, lambda p: val_s.at[p], val_y, sems[4])
     go_val_z = Spread(NZ, z, dev_z, lambda p: val_t.at[p], val_z, sems[5])
-    go_dw_z = Spread(NZ, z, dev_z, lambda p: blk.at[p], dz, sems[6])
+    go_dw_z = Spread(NZ, z, dev_z, lambda p: blk.at[p], dz, sems[6], by_place=True)
     go_sh_x = Spread(NX, x, dev_x, lambda p: shx.at[x], shx, sems[7])
     go_sh_h = Spread(NZH, zh, dev_h, lambda p: shz.at[zh], shz, sems[8])
     go_tab_x = Spread(NX, x, dev_x, lambda p: tab_s.at[p], tab_x, sems[9])
@@ -154,14 +156,12 @@
     core_x = remote(x_hbm, xb.at[pl.ds(ROWS, ROWS)], s_core.at[3], r_core.at[3], partner)
     core_g = remote(g_hbm, gb.at[pl.ds(ROWS, ROWS)], s_core.at[4], r_core.at[4], partner)
 
-    own_hot = hot(own_ref[...] == iota((ENT, 128), 1))
-    earlier = nn(hot(iota((ENT, ENT), 1) < iota((ENT, ENT), 0)), own_hot) * own_hot.astype(F32)
-    place_row = nt(jnp.ones((8, 128), BF16), earlier.astype(BF16))
-    owner_row = nt(iota((8, 128), 1).astype(F32).astype(BF16), own_hot)
+    own_hot = jnp.where(own_ref[...] == iota((128, ENT), 0), 1.0, 0.0)
+    earlier = nn(own_hot.astype(BF16), hot(iota((ENT, ENT), 0) < iota((ENT, ENT), 1)))
     meta[...] = jnp.zeros_like(meta)
     meta[0:1, 0:ROWS] = len_ref[...].astype(F32)
-    meta[1:2, 0:ENT] = owner_row[0:1] * 4.0 + place_row[0:1]
-    meta[2:3, 0:ENT] = row_ref[...].astype(F32)
+    meta[1:2, 0:ENT] = own_ref[...].astype(F32) * 4.0 + jnp.sum(earlier * own_hot, axis=0, keepdims=True)
+    meta[2:3, 0:ENT] = row_ref[...].astype(F32).reshape(1, ENT)
 
     count = cnt_ref[0, 0]
     stat[...] = jnp.zeros_like(stat)
@@ -193,7 +193,8 @@
 
     xt_rows = DIN // 2
     choose_i, choose_k = iota((xt_rows, DIN), 0), iota((xt_rows, DIN), 1)
-    choose = hot(choose_k == (choose_i >> 3) * 16 + c * 8 + (choose_i & 7))
+    wanted = ((choose_i >> 5) & 7) * 128 + (choose_i >> 8) * 64 + ((choose_i >> 3) & 3) * 16 + c * 8 + (choose_i & 7)
+    choose = hot(choose_k == wanted)
 
     core_stat.wait_recv()
     stat_y[y] = stat[c] + stat_c[...]
@@ -269,27 +270,30 @@
         g = gb[rows, :].astype(F32)
         gp[rows, :] = jnp.where(alive, scale * (g - mean_dy - nb[rows, :] * mean_dyx), 0.0).astype(BF16)
 
-    for j in range(DOUT // LOAD):
-        cols = slice(j * LOAD, (j + 1) * LOAD)
-        dw[:, :, :, cols] = nn(xt[...], gp[:, cols]).astype(BF16).reshape(NY, 2, 32, LOAD)
-
     streams = []
     for h in range(2):
         for d in (1, -1):
             streams.append((len(streams), h, d, LONG if (h == 0) == (d == 1) else LONG - 1))
 
     def hop(s, h, d, n, k):
-        src = dw.at[lax.rem(y + d * (n - k) + NY, NY), h] if k == 0 else ring.at[s, k - 1]
+        src = dw.at[h, lax.rem(y + d * (n - k) + NY, NY)] if k == 0 else ring.at[s, k - 1]
         return remote(src, ring.at[s, k], s_ring.at[s, k], r_ring.at[s, k], dev_y(lax.rem(y + d + NY, NY)))
 
-    for s, h, d, n in streams:
-        hop(s, h, d, n, 0).start()
+    quarter = DIN // 4
+    for half in range(2):
+        for j in range(DOUT // LOAD):
+            cols = slice(j * LOAD, (j + 1) * LOAD)
+            part = nn(xt[half * quarter : (half + 1) * quarter, :], gp[:, cols])
+            dw[half, :, :, cols] = part.astype(BF16).reshape(NY, 32, LOAD)
+        for s, h, d, n in streams:
+            if h == half:
+                hop(s, h, d, n, 0).start()
 
     def ring_step(k):
         for s, h, d, n in streams:
             if k < n - 1:
                 hop(s, h, d, n, k).wait_recv()
-                own = dw[lax.rem(y + d * (n - k - 1) + NY, NY), h]
+                own = dw[h, lax.rem(y + d * (n - k - 1) + NY, NY)]
                 ring[s, k] = (ring[s, k].astype(F32) + own.astype(F32)).astype(BF16)
                 hop(s, h, d, n, k + 1).start()
 
@@ -349,16 +353,19 @@
             at_row = i * SLOT + k * 8
             rows_hot[at_row : at_row + 16, :] = hot(at == iota((16, TROWS), 1).astype(F32))
 
-    for s, h, d, n in streams:
-        hop(s, h, d, n, n - 1).wait_recv()
-    for h in range(2):
-        long_s, short_s = (0, 1) if h == 0 else (3, 2)
-        summed = ring[long_s, LONG - 1].astype(F32) + dw[y, h].astype(F32) + ring[short_s, LONG - 2].astype(F32)
+    for half in range(2):
+        for s, h, d, n in streams:
+            if h == half:
+                hop(s, h, d, n, n - 1).wait_recv()
+        long_s, short_s = (0, 1) if half == 0 else (3, 2)
+        summed = ring[long_s, LONG - 1].astype(F32) + dw[half, y].astype(F32) + ring[short_s, LONG - 2].astype(F32)
         for i in range(4):
             b = summed[8 * i : 8 * (i + 1)]
-            blk[4 * h + i] = jnp.concatenate([b[:, 0:HALF], b[:, HALF:DOUT]], axis=0).astype(BF16)
+            blk[4 * half + i] = jnp.concatenate([b[:, 0:HALF], b[:, HALF:DOUT]], axis=0).astype(BF16)
+        for p in range(4 * half, 4 * half + 4):
+            to_p = remote(blk.at[p], dz.at[z], sems[6][0].at[p], sems[6][1].at[z], dev_z(p))
+            pl.when(z != p)(to_p.start)
     dz[z] = blk[z]
-    go_dw_z.start()
 
     go_val_z.wait()
     table = lax.dot_general(
@@ -376,6 +383,10 @@
 
     w_s, w_c = block_of(ws), block_of(wc)
 
+    go_tab_x.wait()
+    tab_h[zh] = total(tab_x, NX).astype(BF16)
+    go_tab_h.start()
+
     go_dw_z.wait()
     summed = total(dz, NZ)
     dw_rows = jnp.concatenate([summed[0:8], summed[8:16]], axis=1)
@@ -384,10 +395,6 @@
     go_sh_x.start()
     dwc_ref[...] = dw_rows * w_s
 
-    go_tab_x.wait()
-    tab_h[zh] = total(tab_x, NX).astype(BF16)
-    go_tab_h.start()
-
     go_sh_x.wait()
     shz[zh] = total(shx, NX).astype(BF16)
     go_sh_h.start()
@@ -399,21 +406,30 @@
     tab_g[x] = total(tab_h, NZH).astype(BF16)
     go_tab_g.start()
 
-    go_sh_h.wait()
-    summed = total(shz, NZH)
-    dws_ref[...] = jnp.concatenate([summed[0:8], summed[8:16]], axis=1)
-
-    go_tab_g.wait()
-    tab_ref[...] = tab_g[...].astype(F32).reshape(TROWS, EMB)
-
     for sp in spreads:
-        sp.finish()
+        if sp not in (go_sh_h, go_tab_g):
+            sp.finish()
     for cp in (core_stat, core_fin, core_meta, core_x, core_g):
         cp.wait_send()
     for s, h, d, n in streams:
         for k in range(n):
             hop(s, h, d, n, k).wait_send()
     out_gi.wait()
+
+    go_sh_h.wait()
+    summed = total(shz, NZH)
+    dws_ref[...] = jnp.concatenate([summed[0:8], summed[8:16]], axis=1)
+
+    go_tab_g.wait()
+    tab_ref[...] = tab_g[...].astype(F32).reshape(TROWS, EMB)
+
+    for sp in (go_sh_h, go_tab_g):
+        sp.finish()
+
+
+def hand_over(*refs):
+    for i in range(6):
+        refs[6 + i][...] = refs[i][...]
 
 
 def per_device(*args):
@@ -428,7 +444,7 @@
         V((DIN, DOUT), BF16), V((2 * ROWS, DOUT), F32), V((2 * ROWS, DOUT), BF16), V((DIN // 2, 2 * ROWS), BF16),
         V((ROWS, DIN), BF16),
         V((2, 8, HALF), F32), V((8, HALF), F32), V((NY, 8, HALF), F32), V((NZ, 8, HALF), F32), V((2, 8, HALF), F32),
-        V((NY, 2, 32, DOUT), BF16), V((4, LONG, 32, DOUT), BF16), V((NZ, 16, HALF), BF16),
+        V((2, NY, 32, DOUT), BF16), V((4, LONG, 32, DOUT), BF16), V((NZ, 16, HALF), BF16),
         V((NZ, 16, HALF), BF16), V((NX, 16, HALF), BF16), V((NZH, 16, HALF), BF16),
         V((8, 512), F32), V((8, 512), F32), V((SLOTS, 2 * ROWS), BF16), V((NY, 8, 128), F32), V((NY, 8, 128), F32),
         V((NZ, 8, 128), F32), V((NZ, 8, 128), F32), V((SLOTS, TROWS), BF16), V((SLOTS, SLOTS), BF16),
@@ -453,8 +469,17 @@
         name="layer_backward",
     )(
         layer_input, grad_output, row_counts, w_shared, w_scen[0], gain_shared.reshape(1, DOUT), gain_scen,
-        saved_mean, saved_rstd, bag_lengths, owner_shard, table_row.reshape(1, ENT),
+        saved_mean, saved_rstd, bag_lengths, owner_shard.reshape(1, ENT), table_row,
     )
+    results = (grad_in, dw_shared, dw_scen, dgain_shared, dgain_scen, table)
+    grad_in, dw_shared, dw_scen, dgain_shared, dgain_scen, table = pl.pallas_call(
+        hand_over,
+        out_shape=tuple(shape(r.shape, r.dtype) for r in results),
+        in_specs=[vm] * 6,
+        out_specs=(vm,) * 6,
+        compiler_params=pltpu.CompilerParams(vmem_limit_bytes=60 << 20),
+        name="hand_over",
+    )(*results)
     return grad_in, dw_shared, dw_scen[None], dgain_shared.reshape(DOUT), dgain_scen, table
 
 

time: 92.9 us -> 80 us (0.86)
  the two profiles are of different devices: /device:TPU:48 before, /device:TPU:8 now
where the time goes in v2:
time: 80 us; the launch traced here: 79.7 us
  Pallas kernels  78.5 us (98%)
  between operations  1.29 us (2%)
    pallas_call x1, Pallas kernels, per_device(): pl.pallas_call(kernel, out_shape=(shape((ROWS, DIN), BF16), shape((8, DOU...  76.4 us
    pallas_call x1, Pallas kernels, per_device(): pl.pallas_call(hand_over, out_shape=tuple((shape(r.shape, r.dtype) for r...  2.09 us

profile of v2, /device:TPU:8, one launch (start us, length us, event | category | flops | bytes accessed | tf_op | source)
XLA Modules:
  0.0 79.7 jit_solution(8445967904467756642)
XLA Ops:
  1.3 76.4 %layer_backward.1 = (bf16[256,1024]{1,0:T(8,128)(2,1)}, f32[8,1024]{1,0:T(8,128)}, f32[8,1024]{1,0:T(8,128)}, f32[8,128]{1,0:T(8,128)}, f32[1,1024]{1,0:T(1,128)}, /*index=5*/f32[512,128]{1,0:T(8,128)}) custom-call(bf16[256,1024]{1,0:T(8,128)(2,1)} %x_hbm.1, bf16[256,1024]{1,0:T(8,128)(2,1)} %g_hbm.1, s32[1,1]{1,0:T(1,128)S(6)} %copy.18.cnt_ref, ...), custom_call_target="tpu_custom_call" | custom-call | tf_op jit(solution)/shard_map/layer_backward/pallas_call | solution.py:459
  77.7 2.1 %hand_over.1 = (bf16[256,1024]{1,0:T(8,128)(2,1)}, f32[8,1024]{1,0:T(8,128)}, f32[8,1024]{1,0:T(8,128)}, f32[8,128]{1,0:T(8,128)}, f32[1,1024]{1,0:T(1,128)}, /*index=5*/f32[512,128]{1,0:T(8,128)}) custom-call(bf16[256,1024]{1,0:T(8,128)(2,1)} %get-tuple-element.18.refs_0_, f32[8,1024]{1,0:T(8,128)} %get-tuple-element.19.refs_1_, ...), custom_call_target="tpu_custom_call" | custom-call | tf_op jit(solution)/shard_map/hand_over/pallas_call | solution.py:475

commit v3 on v2

--- a/solution.py
+++ b/solution.py
@@ -28,16 +28,35 @@
     )
 
 
+def far_first(n, me):
+    return [lax.rem(me + k, n) for k in sorted(range(1, n), key=lambda k: -min(k, n - k))]
+
+
+def far_line(n, me):
+    upper = me // (n // 2)
+    order = []
+    for i in range(n - 1):
+        down = n - 1 - i - (me + i + 1) // n
+        up = i + (i - me + n) // n
+        order.append((1 - upper) * down + upper * up)
+    return order
+
+
 class Spread:
-    def __init__(self, n, me, dev, src_of, buf, sems, by_place=False):
+    def __init__(self, n, me, dev, src_of, buf, sems, by_place=False, line=False):
         self.n, self.me, self.dev, self.src_of, self.buf = n, me, dev, src_of, buf
         self.send, self.recv = sems
         self.by_place = by_place
+        self.order = far_line(n, me) if line else far_first(n, me)
+
+    def sends(self):
+        for i, p in enumerate(self.order):
+            sem = self.send.at[p if self.by_place else i + 1]
+            yield remote(self.src_of(p), self.buf.at[self.me], sem, self.recv.at[self.me], self.dev(p))
 
     def start(self):
-        for k in range(1, self.n):
-            p = lax.rem(self.me + k, self.n)
-            remote(self.src_of(p), self.buf.at[self.me], self.send.at[k], self.recv.at[self.me], self.dev(p)).start()
+        for cp in self.sends():
+            cp.start()
 
     def wait(self):
         for k in range(1, self.n):
@@ -45,10 +64,8 @@
             remote(self.buf.at[q], self.buf.at[q], self.send.at[k], self.recv.at[q], self.dev(q)).wait_recv()
 
     def finish(self):
-        for k in range(1, self.n):
-            p = lax.rem(self.me + k, self.n)
-            sem = self.send.at[p if self.by_place else k]
-            remote(self.src_of(p), self.buf.at[self.me], sem, self.recv.at[self.me], self.dev(p)).wait_send()
+        for cp in self.sends():
+            cp.wait_send()
 
 
 def nt(a, b):
@@ -103,6 +120,15 @@
 
     other = 1 - c
     partner = (scen, (y * NZ + z) * 2 + other)
+
+    barrier = pltpu.get_barrier_semaphore()
+    peers = [dev_h(1 - zh)]
+    peers += [dev_z(lax.rem(z + k, NZ)) for k in range(1, NZ)]
+    peers += [dev_y(lax.rem(y + k, NY)) for k in range(1, NY)]
+    peers += [dev_x(lax.rem(x + k, NX)) for k in range(1, NX)]
+    peers += [partner]
+    for p in peers:
+        pl.semaphore_signal(barrier, 1, device_id=p, device_id_type=pl.DeviceIdType.MESH)
 
     in_x = pltpu.make_async_copy(x_hbm, xb.at[pl.ds(0, ROWS)], s_load.at[0])
     in_g = pltpu.make_async_copy(g_hbm, gb.at[pl.ds(0, ROWS)], s_load.at[1])
@@ -123,23 +149,14 @@
         a.start()
         b.start()
 
-    barrier = pltpu.get_barrier_semaphore()
-    peers = [dev_h(1 - zh)]
-    peers += [dev_z(lax.rem(z + k, NZ)) for k in range(1, NZ)]
-    peers += [dev_y(lax.rem(y + k, NY)) for k in range(1, NY)]
-    peers += [dev_x(lax.rem(x + k, NX)) for k in range(1, NX)]
-    peers += [partner]
-    for p in peers:
-        pl.semaphore_signal(barrier, 1, device_id=p, device_id_type=pl.DeviceIdType.MESH)
-
     sems = [(spread_sems[2 * i], spread_sems[2 * i + 1]) for i in range(len(spread_sems) // 2)]
     go_stat_y = Spread(NY, y, dev_y, lambda p: stat_y.at[y], stat_y, sems[0])
-    go_stat_z = Spread(NZ, z, dev_z, lambda p: stat_z.at[z], stat_z, sems[1])
+    go_stat_z = Spread(NZ, z, dev_z, lambda p: stat_z.at[z], stat_z, sems[1], line=True)
     go_ids_y = Spread(NY, y, dev_y, lambda p: ids_s.at[p], ids_y, sems[2])
-    go_ids_z = Spread(NZ, z, dev_z, lambda p: ids_t.at[p], ids_z, sems[3])
+    go_ids_z = Spread(NZ, z, dev_z, lambda p: ids_t.at[p], ids_z, sems[3], line=True)
     go_val_y = Spread(NY, y, dev_y, lambda p: val_s.at[p], val_y, sems[4])
-    go_val_z = Spread(NZ, z, dev_z, lambda p: val_t.at[p], val_z, sems[5])
-    go_dw_z = Spread(NZ, z, dev_z, lambda p: blk.at[p], dz, sems[6], by_place=True)
+    go_val_z = Spread(NZ, z, dev_z, lambda p: val_t.at[p], val_z, sems[5], line=True)
+    go_dw_z = Spread(NZ, z, dev_z, lambda p: blk.at[p], dz, sems[6], by_place=True, line=True)
     go_sh_x = Spread(NX, x, dev_x, lambda p: shx.at[x], shx, sems[7])
     go_sh_h = Spread(NZH, zh, dev_h, lambda p: shz.at[zh], shz, sems[8])
     go_tab_x = Spread(NX, x, dev_x, lambda p: tab_s.at[p], tab_x, sems[9])
@@ -162,6 +179,27 @@
     meta[0:1, 0:ROWS] = len_ref[...].astype(F32)
     meta[1:2, 0:ENT] = own_ref[...].astype(F32) * 4.0 + jnp.sum(earlier * own_hot, axis=0, keepdims=True)
     meta[2:3, 0:ENT] = row_ref[...].astype(F32).reshape(1, ENT)
+
+    def slots_of(m, src):
+        lens = m[0:1, 0:ROWS]
+        upto = hot(iota((ROWS, ROWS), 0) <= iota((ROWS, ROWS), 1))
+        ends = nn(jnp.broadcast_to(lens, (8, ROWS)).astype(BF16), upto)[0:1]
+        entry = iota((ENT, ROWS), 0).astype(F32)
+        picker = hot((ends > entry) & (ends - lens <= entry))
+        code = m[1:2, 0:ENT].astype(I32)
+        owner, place = code >> 2, code & 3
+        inside = src * PART + ((owner >> 1) & 7) * CAP + place
+        mine = (owner & 1) == c
+        slot = jnp.where(mine, (owner >> 4) * SLOT + inside, -1)
+        wide = jnp.where(mine, (owner >> 4) * 128 + inside, -1)
+        chosen = nn(hot(iota((SLOTS, ENT), 0) == slot), picker).astype(BF16)
+        name = m[2:3, 0:ENT].astype(I32) + 1
+        part = jnp.where(iota((8, ENT), 0) == 0, name >> 4, name & 15)
+        names = nt(part.astype(F32).astype(BF16), hot(iota((NY * 128, ENT), 0) == wide))
+        return chosen, names
+
+    chosen, names = slots_of(meta, c)
+    pick[:, 0:ROWS] = chosen
 
     count = cnt_ref[0, 0]
     stat[...] = jnp.zeros_like(stat)
@@ -202,27 +240,7 @@
 
     xt[:, 0:ROWS] = nt(choose, xb[0:ROWS, :]).astype(BF16)
 
-    def slots_of(m, src):
-        lens = m[0:1, 0:ROWS]
-        upto = hot(iota((ROWS, ROWS), 0) <= iota((ROWS, ROWS), 1))
-        ends = nn(jnp.broadcast_to(lens, (8, ROWS)).astype(BF16), upto)[0:1]
-        entry = iota((ENT, ROWS), 0).astype(F32)
-        picker = hot((ends > entry) & (ends - lens <= entry))
-        code = m[1:2, 0:ENT].astype(I32)
-        owner, place = code >> 2, code & 3
-        inside = src * PART + ((owner >> 1) & 7) * CAP + place
-        mine = (owner & 1) == c
-        slot = jnp.where(mine, (owner >> 4) * SLOT + inside, -1)
-        wide = jnp.where(mine, (owner >> 4) * 128 + inside, -1)
-        chosen = nn(hot(iota((SLOTS, ENT), 0) == slot), picker).astype(BF16)
-        name = m[2:3, 0:ENT].astype(I32) + 1
-        part = jnp.where(iota((8, ENT), 0) == 0, name >> 4, name & 15)
-        names = nt(part.astype(F32).astype(BF16), hot(iota((NY * 128, ENT), 0) == wide))
-        return chosen, names
-
     core_meta.wait_recv()
-    chosen, names = slots_of(meta, c)
-    pick[:, 0:ROWS] = chosen
     chosen, names_p = slots_of(meta_p, other)
     pick[:, ROWS : 2 * ROWS] = chosen
     names = names + names_p
@@ -240,12 +258,6 @@
     for j in range(loads):
         cols = pl.ds(j * LOAD, LOAD)
         nb[ROWS : 2 * ROWS, cols] = (nn(xb[ROWS : 2 * ROWS, :], we[:, cols]) - mean_ref[:, cols]) * rstd_ref[:, cols]
-    out_i, in_i = iota((SLOTS, SLOTS), 0), iota((SLOTS, SLOTS), 1)
-    to_z = (out_i * 1366) >> 16
-    in_z = out_i - to_z * SLOT
-    six, from_y = in_z >> 3, in_z & 7
-    src_c = jnp.where(six >= CAP, 1, 0)
-    perm[...] = hot(in_i == from_y * SLOT + src_c * PART + to_z * CAP + six - CAP * src_c)
     core_g.wait_recv()
 
     go_stat_z.wait()
@@ -301,6 +313,12 @@
     val_s[...] = nn(pick[...], pooled).astype(BF16).reshape(NY, SLOT, EMB)
     val_y[y] = val_s[y]
     go_val_y.start()
+    out_i, in_i = iota((SLOTS, SLOTS), 0), iota((SLOTS, SLOTS), 1)
+    to_z = (out_i * 1366) >> 16
+    in_z = out_i - to_z * SLOT
+    six, from_y = in_z >> 3, in_z & 7
+    src_c = jnp.where(six >= CAP, 1, 0)
+    perm[...] = hot(in_i == from_y * SLOT + src_c * PART + to_z * CAP + six - CAP * src_c)
 
     dgc_ref[...] = gs_ref[...] * sum_dyx
     gain_term = gc_ref[...] * sum_dyx

time: 80 us -> 79.4 us (level)
  the two profiles are of different devices: /device:TPU:8 before, /device:TPU:2 now
where the time goes in v3:
time: 79.4 us; the launch traced here: 79.2 us
  Pallas kernels  77.9 us (98%)
  between operations  1.29 us (2%)
    pallas_call x1, Pallas kernels, per_device(): pl.pallas_call(kernel, out_shape=(shape((ROWS, DIN), BF16), shape((8, DOU...  75.8 us
    pallas_call x1, Pallas kernels, per_device(): pl.pallas_call(hand_over, out_shape=tuple((shape(r.shape, r.dtype) for r...  2.09 us

profile of v3, /device:TPU:2, one launch (start us, length us, event | category | flops | bytes accessed | tf_op | source)
XLA Modules:
  0.0 79.2 jit_solution(6791624695372481454)
XLA Ops:
  1.3 75.8 %layer_backward.1 = (bf16[256,1024]{1,0:T(8,128)(2,1)}, f32[8,1024]{1,0:T(8,128)}, f32[8,1024]{1,0:T(8,128)}, f32[8,128]{1,0:T(8,128)}, f32[1,1024]{1,0:T(1,128)}, /*index=5*/f32[512,128]{1,0:T(8,128)}) custom-call(bf16[256,1024]{1,0:T(8,128)(2,1)} %x_hbm.1, bf16[256,1024]{1,0:T(8,128)(2,1)} %g_hbm.1, s32[1,1]{1,0:T(1,128)S(6)} %copy.18.cnt_ref, ...), custom_call_target="tpu_custom_call" | custom-call | tf_op jit(solution)/shard_map/layer_backward/pallas_call | solution.py:477
  77.1 2.1 %hand_over.1 = (bf16[256,1024]{1,0:T(8,128)(2,1)}, f32[8,1024]{1,0:T(8,128)}, f32[8,1024]{1,0:T(8,128)}, f32[8,128]{1,0:T(8,128)}, f32[1,1024]{1,0:T(1,128)}, /*index=5*/f32[512,128]{1,0:T(8,128)}) custom-call(bf16[256,1024]{1,0:T(8,128)(2,1)} %get-tuple-element.18.refs_0_, f32[8,1024]{1,0:T(8,128)} %get-tuple-element.19.refs_1_, ...), custom_call_target="tpu_custom_call" | custom-call | tf_op jit(solution)/shard_map/hand_over/pallas_call | solution.py:493
